TPU v7x, 32 devices: a whole 2x2x4 slice. The times are simulated.
32 devices in a mesh: groups: 2 (over x), ctx: 8 (over z, y), tp: 2 (over core).
Axes of the slice: x: 2, y: 2, z: 4, core: 2. Of those that a mesh axis runs over, the one named last changes fastest.
Arguments:
- queries: bfloat16 [3072, 4096], P(('groups', 'ctx'), 'tp'), parts along dimension 0, may hold values from -400 to 400
- keys: bfloat16 [3072, 512], P(('groups', 'ctx'), 'tp'), parts along dimension 0, may hold values from -400 to 400
- values: bfloat16 [3072, 512], P(('groups', 'ctx'), 'tp'), parts along dimension 0, may hold values from -6 to 6
- q_gain: float32 [128], replicated, may hold values from 1 to 5
- k_gain: float32 [128], replicated, may hold values from 1 to 5
- counts: int32 [16], P('groups'), parts along dimension 0, may hold values from 48 to 192, as said below
Outputs:
- attended: bfloat16 [3072, 4096], P(('groups', 'ctx'), 'tp'), parts along dimension 0
There are 2 independent parts, one for each index of `groups`. A program takes and returns all parts, laid end to end along the dimension named above; an argument that names none is the same for every part. Nothing has to cross between parts.
Inputs may be any that keep to these rules, and one draw needn't show every extreme that they name: `counts`: some block has all 192 tokens live and some block only 48.
All inputs are finite; a program needn't handle non-finite values.
Results may differ from a plain program's by a relative error of at most 0.004.
The roundings to bfloat16 on the way count: a program that leaves them out, or rounds other values in their place, can miss the bound.
Values may be sent and summed in bfloat16 or wider, within the bound.
A program may use at most 64 MiB of HBM per device.

v0:
```python
import math

import jax
import jax.numpy as jnp
from jax import lax
from jax.sharding import PartitionSpec as P


def rope_tables(positions, head_width):
    frequency = jnp.power(
        jnp.float32(1000000.0), -jnp.arange(0, head_width, 2).astype(jnp.float32) / head_width
    )
    angles = positions.astype(jnp.float32)[:, None] * frequency[None, :]
    cosine_table = jnp.cos(angles)
    sine_table = jnp.sin(angles)
    return (
        jnp.concatenate([cosine_table, cosine_table], 1),
        jnp.concatenate([sine_table, sine_table], 1),
    )


def norm_rope(inputs, gain, positions, head_width):
    row_count = inputs.shape[0]
    head_count = inputs.shape[1] // head_width
    normed = inputs.astype(jnp.float32).reshape(row_count, head_count, head_width)
    normed = normed * lax.rsqrt(jnp.mean(normed * normed, -1, keepdims=True) + 1e-06) * gain
    cosine_table, sine_table = rope_tables(positions, head_width)
    turned = jnp.concatenate([-normed[..., head_width // 2 :], normed[..., : head_width // 2]], -1)
    rotated = normed * cosine_table[:, None, :] + turned * sine_table[:, None, :]
    return rotated.astype(jnp.bfloat16)


def lookup(table, index_rows):
    hits = index_rows[:, None] == jnp.arange(table.shape[0], dtype=jnp.int32)[None, :]
    return jnp.sum(jnp.where(hits, table[None, :], 0), 1)


def local(queries, keys, values, q_gain, k_gain, counts):
    shard_rows = queries.shape[0]
    half_rows = shard_rows // 2
    head_width = q_gain.shape[0]
    q_heads = queries.shape[1] // head_width
    kv_heads = keys.shape[1] // head_width
    group_size = q_heads // kv_heads
    ctx_index = lax.axis_index("ctx")
    local_index = jnp.arange(shard_rows, dtype=jnp.int32)
    query_pos = ctx_index * shard_rows + local_index
    query_live = query_pos % shard_rows < lookup(counts, query_pos // shard_rows)
    q_ready = norm_rope(queries, q_gain, query_pos, head_width).reshape(
        shard_rows, kv_heads, group_size, head_width
    )
    k_ready = norm_rope(keys, k_gain, query_pos, head_width).reshape(
        shard_rows, kv_heads * head_width
    )
    score_scale = head_width ** (-0.5)
    halves = [
        (q_ready[:half_rows], query_pos[:half_rows]),
        (q_ready[half_rows:], query_pos[half_rows:]),
    ]
    start_state = (
        jnp.full((kv_heads, group_size, half_rows), -1e30, jnp.float32),
        jnp.zeros((kv_heads, group_size, half_rows), jnp.float32),
        jnp.zeros((kv_heads, group_size, half_rows, head_width), jnp.float32),
    )
    key_piece = lax.all_gather(k_ready, "ctx", axis=0, tiled=True)
    val_piece = lax.all_gather(values, "ctx", axis=0, tiled=True)
    length = key_piece.shape[0]
    block_size = math.gcd(length, shard_rows)
    block_count = length // block_size
    key_blocks = key_piece.reshape(block_count, block_size, kv_heads, head_width)
    val_blocks = val_piece.reshape(block_count, block_size, kv_heads, head_width)

    def step(carried, scan_item):
        key_block, val_block, block_index = scan_item
        key_pos = block_index * block_size + jnp.arange(block_size, dtype=jnp.int32)
        key_live = key_pos % shard_rows < lookup(counts, key_pos // shard_rows)
        updated = []
        for (query_half, half_pos), half_state in zip(halves, carried):

            def update(
                state_now,
                query_half=query_half,
                half_pos=half_pos,
                key_block=key_block,
                val_block=val_block,
                key_pos=key_pos,
                key_live=key_live,
            ):
                old_max, old_total, old_sum = state_now
                scores = (
                    jnp.einsum(
                        "qkgd,skd->kgqs", query_half, key_block, preferred_element_type=jnp.float32
                    )
                    * score_scale
                )
                allowed = key_live[None, :] & (key_pos[None, :] <= half_pos[:, None])
                scores = jnp.where(allowed[None, None], scores, -1e30)
                new_max = jnp.maximum(old_max, jnp.max(scores, -1))
                weights = jnp.where(allowed[None, None], jnp.exp(scores - new_max[..., None]), 0.0)
                rescale = jnp.exp(old_max - new_max)
                new_total = old_total * rescale + jnp.sum(weights, -1)
                new_sum = old_sum * rescale[..., None] + jnp.einsum(
                    "kgqs,skd->kgqd",
                    weights.astype(jnp.bfloat16),
                    val_block,
                    preferred_element_type=jnp.float32,
                )
                return (new_max, new_total, new_sum)

            needed = jnp.any(key_live & (key_pos <= jnp.max(half_pos)))
            updated.append(lax.cond(needed, update, lambda state_now: state_now, half_state))
        return (tuple(updated), None)

    carried, _ = lax.scan(
        step,
        (start_state, start_state),
        (key_blocks, val_blocks, jnp.arange(block_count, dtype=jnp.int32)),
    )
    outputs = []
    for half_state in carried:
        summed = half_state[2] / half_state[1][..., None]
        outputs.append(jnp.transpose(summed, (2, 0, 1, 3)).reshape(half_rows, q_heads * head_width))
    attended = jnp.where(query_live[:, None], jnp.concatenate(outputs, 0), 0.0).astype(jnp.bfloat16)
    return attended


def solution(mesh):
    in_specs = (
        P(("groups", "ctx"), "tp"),
        P(("groups", "ctx"), "tp"),
        P(("groups", "ctx"), "tp"),
        P(),
        P(),
        P("groups"),
    )
    out_specs = P(("groups", "ctx"), "tp")
    return jax.shard_map(local, mesh=mesh, in_specs=in_specs, out_specs=out_specs, check_vma=False)
```

profile of v0, /device:TPU:28, one launch (start us, length us, event | category | flops | bytes accessed | tf_op | source)
XLA Modules:
  0.0 149.4 jit_solution(3002761306145389188)
XLA Ops:
  0.6 1.3 convert_bitcast_fusion
  3.9 1.0 fusion.22
  7.5 32.1 %all_gather.6 = bf16[1536,256]{1,0:T(8,128)(2,1)S(1)} all-gather(bf16[192,256]{1,0:T(8,128)(2,1)S(1)} %fusion.24), channel_id=1, replica_groups=mesh['groups'=2,'ctx'=8,'tp'=2] {'ctx'}, dimensions={0}, use_global_device_ids=true | all-gather | bytes 884736 | tf_op jit(solution)/shard_map/all_gather | solution.py:65
  40.6 32.0 %all_gather.7 = bf16[1536,256]{1,0:T(8,128)(2,1)S(1)} all-gather(bf16[192,256]{1,0:T(8,128)(2,1)S(1)} %copy-done.1), channel_id=1, replica_groups=mesh['groups'=2,'ctx'=8,'tp'=2] {'ctx'}, dimensions={0}, use_global_device_ids=true | all-gather | bytes 884736 | tf_op jit(solution)/shard_map/all_gather | solution.py:66
  72.5 1.1 reshape.193
  73.8 73.3 %while.22 = (s32[]{:T(128)}, f32[2,8,96]{2,1,0:T(8,128)S(1)}, f32[2,8,96]{2,1,0:T(8,128)S(1)}, f32[2,8,96,128]{3,2,1,0:T(8,128)S(1)}, f32[2,8,96]{2,1,0:T(8,128)...) while((s32[]{:T(128)}, f32[2,8,96]{2,1,0:T(8,128)S(1)}, ...), condition=%wide.region_17.18_spmd, body=%wide.region_5.17_spmd.sunk | while | flops 308173440 | bytes 12540997 | solution.py:114
  75.1 2.0 %and_reduce_fusion.3 = (pred[]{:T(512)}, pred[]{:T(512)}, pred[192]{0:T(512)(128)(4,1)S(1)}) fusion(s32[]{:T(128)} %get-tuple-element.639, s32[]{:T(128)} %bitcast.81, s32[]{:T(128)} %get-tuple-element.634, s32[192]{0:T(256)S(1)} %select_reduce_fusion.3), kind=kLoop, calls=%fused_computation.32.clone.1 | loop fusion | flops 2686 | bytes 974 | tf_op jit(solution)/shard_map/while/body/eval_jaxpr/reduce_or | solution.py:110
  78.8 1.7 %conditional.5 = ((f32[2,8,96]{2,1,0:T(8,128)S(1)}, f32[2,8,96]{2,1,0:T(8,128)S(1)}, f32[2,8,96,128]{3,2,1,0:T(8,128)S(1)})) conditional(s32[]{:T(128)} %convert_element_type.67, (f32[2,8,96]{2,1,0:T(8,128)S(1)}, f32[2,8,96]{2,1,0:T(8,128)S(1)}, f32[2,8,96,128]{3,2,1,0:T(8,128)S(1)}) %tuple.74, (pred[192]{0:T(512)(128)(4,1)S(1)}, ...), branch_computations={%region_13.13_spmd, %region_14.16_spmd} | conditional | flops 154082304 | bytes 5875040 | solution.py:111
  81.2 1.7 %conditional.4 = ((f32[2,8,96]{2,1,0:T(8,128)S(1)}, f32[2,8,96]{2,1,0:T(8,128)S(1)}, f32[2,8,96,128]{3,2,1,0:T(8,128)S(1)})) conditional(s32[]{:T(128)} %convert_element_type.66, (f32[2,8,96]{2,1,0:T(8,128)S(1)}, f32[2,8,96]{2,1,0:T(8,128)S(1)}, f32[2,8,96,128]{3,2,1,0:T(8,128)S(1)}) %tuple.72, (pred[192]{0:T(512)(128)(4,1)S(1)}, s32[192]{0:T(256)S(1)}, ...), branch_computations={%region_8.8_spmd, %region_9.11_spmd} | conditional | flops 154082304 | bytes 5875040 | solution.py:111
  84.3 2.0 %and_reduce_fusion.3 = (pred[]{:T(512)}, pred[]{:T(512)}, pred[192]{0:T(512)(128)(4,1)S(1)}) fusion(s32[]{:T(128)} %get-tuple-element.639, s32[]{:T(128)} %bitcast.81, s32[]{:T(128)} %get-tuple-element.634, s32[192]{0:T(256)S(1)} %select_reduce_fusion.3), kind=kLoop, calls=%fused_computation.32.clone.1 | loop fusion | flops 2686 | bytes 974 | tf_op jit(solution)/shard_map/while/body/eval_jaxpr/reduce_or | solution.py:110
  86.2 1.0 constant_dynamic-slice_fusion.3
  88.0 1.7 %conditional.5 = ((f32[2,8,96]{2,1,0:T(8,128)S(1)}, f32[2,8,96]{2,1,0:T(8,128)S(1)}, f32[2,8,96,128]{3,2,1,0:T(8,128)S(1)})) conditional(s32[]{:T(128)} %convert_element_type.67, (f32[2,8,96]{2,1,0:T(8,128)S(1)}, f32[2,8,96]{2,1,0:T(8,128)S(1)}, f32[2,8,96,128]{3,2,1,0:T(8,128)S(1)}) %tuple.74, (pred[192]{0:T(512)(128)(4,1)S(1)}, ...), branch_computations={%region_13.13_spmd, %region_14.16_spmd} | conditional | flops 154082304 | bytes 5875040 | solution.py:111
  90.3 1.7 %conditional.4 = ((f32[2,8,96]{2,1,0:T(8,128)S(1)}, f32[2,8,96]{2,1,0:T(8,128)S(1)}, f32[2,8,96,128]{3,2,1,0:T(8,128)S(1)})) conditional(s32[]{:T(128)} %convert_element_type.66, (f32[2,8,96]{2,1,0:T(8,128)S(1)}, f32[2,8,96]{2,1,0:T(8,128)S(1)}, f32[2,8,96,128]{3,2,1,0:T(8,128)S(1)}) %tuple.72, (pred[192]{0:T(512)(128)(4,1)S(1)}, s32[192]{0:T(256)S(1)}, ...), branch_computations={%region_8.8_spmd, %region_9.11_spmd} | conditional | flops 154082304 | bytes 5875040 | solution.py:111
  93.5 2.0 %and_reduce_fusion.3 = (pred[]{:T(512)}, pred[]{:T(512)}, pred[192]{0:T(512)(128)(4,1)S(1)}) fusion(s32[]{:T(128)} %get-tuple-element.639, s32[]{:T(128)} %bitcast.81, s32[]{:T(128)} %get-tuple-element.634, s32[192]{0:T(256)S(1)} %select_reduce_fusion.3), kind=kLoop, calls=%fused_computation.32.clone.1 | loop fusion | flops 2686 | bytes 974 | tf_op jit(solution)/shard_map/while/body/eval_jaxpr/reduce_or | solution.py:110
  97.1 1.7 %conditional.5 = ((f32[2,8,96]{2,1,0:T(8,128)S(1)}, f32[2,8,96]{2,1,0:T(8,128)S(1)}, f32[2,8,96,128]{3,2,1,0:T(8,128)S(1)})) conditional(s32[]{:T(128)} %convert_element_type.67, (f32[2,8,96]{2,1,0:T(8,128)S(1)}, f32[2,8,96]{2,1,0:T(8,128)S(1)}, f32[2,8,96,128]{3,2,1,0:T(8,128)S(1)}) %tuple.74, (pred[192]{0:T(512)(128)(4,1)S(1)}, ...), branch_computations={%region_13.13_spmd, %region_14.16_spmd} | conditional | flops 154082304 | bytes 5875040 | solution.py:111
  99.5 1.7 %conditional.4 = ((f32[2,8,96]{2,1,0:T(8,128)S(1)}, f32[2,8,96]{2,1,0:T(8,128)S(1)}, f32[2,8,96,128]{3,2,1,0:T(8,128)S(1)})) conditional(s32[]{:T(128)} %convert_element_type.66, (f32[2,8,96]{2,1,0:T(8,128)S(1)}, f32[2,8,96]{2,1,0:T(8,128)S(1)}, f32[2,8,96,128]{3,2,1,0:T(8,128)S(1)}) %tuple.72, (pred[192]{0:T(512)(128)(4,1)S(1)}, s32[192]{0:T(256)S(1)}, ...), branch_computations={%region_8.8_spmd, %region_9.11_spmd} | conditional | flops 154082304 | bytes 5875040 | solution.py:111
  102.6 2.0 %and_reduce_fusion.3 = (pred[]{:T(512)}, pred[]{:T(512)}, pred[192]{0:T(512)(128)(4,1)S(1)}) fusion(s32[]{:T(128)} %get-tuple-element.639, s32[]{:T(128)} %bitcast.81, s32[]{:T(128)} %get-tuple-element.634, s32[192]{0:T(256)S(1)} %select_reduce_fusion.3), kind=kLoop, calls=%fused_computation.32.clone.1 | loop fusion | flops 2686 | bytes 974 | tf_op jit(solution)/shard_map/while/body/eval_jaxpr/reduce_or | solution.py:110
  106.3 1.7 %conditional.5 = ((f32[2,8,96]{2,1,0:T(8,128)S(1)}, f32[2,8,96]{2,1,0:T(8,128)S(1)}, f32[2,8,96,128]{3,2,1,0:T(8,128)S(1)})) conditional(s32[]{:T(128)} %convert_element_type.67, (f32[2,8,96]{2,1,0:T(8,128)S(1)}, f32[2,8,96]{2,1,0:T(8,128)S(1)}, f32[2,8,96,128]{3,2,1,0:T(8,128)S(1)}) %tuple.74, (pred[192]{0:T(512)(128)(4,1)S(1)}, ...), branch_computations={%region_13.13_spmd, %region_14.16_spmd} | conditional | flops 154082304 | bytes 5875040 | solution.py:111
  108.7 1.7 %conditional.4 = ((f32[2,8,96]{2,1,0:T(8,128)S(1)}, f32[2,8,96]{2,1,0:T(8,128)S(1)}, f32[2,8,96,128]{3,2,1,0:T(8,128)S(1)})) conditional(s32[]{:T(128)} %convert_element_type.66, (f32[2,8,96]{2,1,0:T(8,128)S(1)}, f32[2,8,96]{2,1,0:T(8,128)S(1)}, f32[2,8,96,128]{3,2,1,0:T(8,128)S(1)}) %tuple.72, (pred[192]{0:T(512)(128)(4,1)S(1)}, s32[192]{0:T(256)S(1)}, ...), branch_computations={%region_8.8_spmd, %region_9.11_spmd} | conditional | flops 154082304 | bytes 5875040 | solution.py:111
  111.8 2.0 %and_reduce_fusion.3 = (pred[]{:T(512)}, pred[]{:T(512)}, pred[192]{0:T(512)(128)(4,1)S(1)}) fusion(s32[]{:T(128)} %get-tuple-element.639, s32[]{:T(128)} %bitcast.81, s32[]{:T(128)} %get-tuple-element.634, s32[192]{0:T(256)S(1)} %select_reduce_fusion.3), kind=kLoop, calls=%fused_computation.32.clone.1 | loop fusion | flops 2686 | bytes 974 | tf_op jit(solution)/shard_map/while/body/eval_jaxpr/reduce_or | solution.py:110
  115.4 1.7 %conditional.5 = ((f32[2,8,96]{2,1,0:T(8,128)S(1)}, f32[2,8,96]{2,1,0:T(8,128)S(1)}, f32[2,8,96,128]{3,2,1,0:T(8,128)S(1)})) conditional(s32[]{:T(128)} %convert_element_type.67, (f32[2,8,96]{2,1,0:T(8,128)S(1)}, f32[2,8,96]{2,1,0:T(8,128)S(1)}, f32[2,8,96,128]{3,2,1,0:T(8,128)S(1)}) %tuple.74, (pred[192]{0:T(512)(128)(4,1)S(1)}, ...), branch_computations={%region_13.13_spmd, %region_14.16_spmd} | conditional | flops 154082304 | bytes 5875040 | solution.py:111
  117.8 1.7 %conditional.4 = ((f32[2,8,96]{2,1,0:T(8,128)S(1)}, f32[2,8,96]{2,1,0:T(8,128)S(1)}, f32[2,8,96,128]{3,2,1,0:T(8,128)S(1)})) conditional(s32[]{:T(128)} %convert_element_type.66, (f32[2,8,96]{2,1,0:T(8,128)S(1)}, f32[2,8,96]{2,1,0:T(8,128)S(1)}, f32[2,8,96,128]{3,2,1,0:T(8,128)S(1)}) %tuple.72, (pred[192]{0:T(512)(128)(4,1)S(1)}, s32[192]{0:T(256)S(1)}, ...), branch_computations={%region_8.8_spmd, %region_9.11_spmd} | conditional | flops 154082304 | bytes 5875040 | solution.py:111
  120.9 2.0 %and_reduce_fusion.3 = (pred[]{:T(512)}, pred[]{:T(512)}, pred[192]{0:T(512)(128)(4,1)S(1)}) fusion(s32[]{:T(128)} %get-tuple-element.639, s32[]{:T(128)} %bitcast.81, s32[]{:T(128)} %get-tuple-element.634, s32[192]{0:T(256)S(1)} %select_reduce_fusion.3), kind=kLoop, calls=%fused_computation.32.clone.1 | loop fusion | flops 2686 | bytes 974 | tf_op jit(solution)/shard_map/while/body/eval_jaxpr/reduce_or | solution.py:110
  124.6 1.7 %conditional.5 = ((f32[2,8,96]{2,1,0:T(8,128)S(1)}, f32[2,8,96]{2,1,0:T(8,128)S(1)}, f32[2,8,96,128]{3,2,1,0:T(8,128)S(1)})) conditional(s32[]{:T(128)} %convert_element_type.67, (f32[2,8,96]{2,1,0:T(8,128)S(1)}, f32[2,8,96]{2,1,0:T(8,128)S(1)}, f32[2,8,96,128]{3,2,1,0:T(8,128)S(1)}) %tuple.74, (pred[192]{0:T(512)(128)(4,1)S(1)}, ...), branch_computations={%region_13.13_spmd, %region_14.16_spmd} | conditional | flops 154082304 | bytes 5875040 | solution.py:111
  127.0 1.7 %conditional.4 = ((f32[2,8,96]{2,1,0:T(8,128)S(1)}, f32[2,8,96]{2,1,0:T(8,128)S(1)}, f32[2,8,96,128]{3,2,1,0:T(8,128)S(1)})) conditional(s32[]{:T(128)} %convert_element_type.66, (f32[2,8,96]{2,1,0:T(8,128)S(1)}, f32[2,8,96]{2,1,0:T(8,128)S(1)}, f32[2,8,96,128]{3,2,1,0:T(8,128)S(1)}) %tuple.72, (pred[192]{0:T(512)(128)(4,1)S(1)}, s32[192]{0:T(256)S(1)}, ...), branch_computations={%region_8.8_spmd, %region_9.11_spmd} | conditional | flops 154082304 | bytes 5875040 | solution.py:111
  130.1 2.0 %and_reduce_fusion.3 = (pred[]{:T(512)}, pred[]{:T(512)}, pred[192]{0:T(512)(128)(4,1)S(1)}) fusion(s32[]{:T(128)} %get-tuple-element.639, s32[]{:T(128)} %bitcast.81, s32[]{:T(128)} %get-tuple-element.634, s32[192]{0:T(256)S(1)} %select_reduce_fusion.3), kind=kLoop, calls=%fused_computation.32.clone.1 | loop fusion | flops 2686 | bytes 974 | tf_op jit(solution)/shard_map/while/body/eval_jaxpr/reduce_or | solution.py:110
  133.8 1.7 %conditional.5 = ((f32[2,8,96]{2,1,0:T(8,128)S(1)}, f32[2,8,96]{2,1,0:T(8,128)S(1)}, f32[2,8,96,128]{3,2,1,0:T(8,128)S(1)})) conditional(s32[]{:T(128)} %convert_element_type.67, (f32[2,8,96]{2,1,0:T(8,128)S(1)}, f32[2,8,96]{2,1,0:T(8,128)S(1)}, f32[2,8,96,128]{3,2,1,0:T(8,128)S(1)}) %tuple.74, (pred[192]{0:T(512)(128)(4,1)S(1)}, ...), branch_computations={%region_13.13_spmd, %region_14.16_spmd} | conditional | flops 154082304 | bytes 5875040 | solution.py:111
  136.2 1.7 %conditional.4 = ((f32[2,8,96]{2,1,0:T(8,128)S(1)}, f32[2,8,96]{2,1,0:T(8,128)S(1)}, f32[2,8,96,128]{3,2,1,0:T(8,128)S(1)})) conditional(s32[]{:T(128)} %convert_element_type.66, (f32[2,8,96]{2,1,0:T(8,128)S(1)}, f32[2,8,96]{2,1,0:T(8,128)S(1)}, f32[2,8,96,128]{3,2,1,0:T(8,128)S(1)}) %tuple.72, (pred[192]{0:T(512)(128)(4,1)S(1)}, s32[192]{0:T(256)S(1)}, ...), branch_computations={%region_8.8_spmd, %region_9.11_spmd} | conditional | flops 154082304 | bytes 5875040 | solution.py:111
  139.3 2.0 %and_reduce_fusion.3 = (pred[]{:T(512)}, pred[]{:T(512)}, pred[192]{0:T(512)(128)(4,1)S(1)}) fusion(s32[]{:T(128)} %get-tuple-element.639, s32[]{:T(128)} %bitcast.81, s32[]{:T(128)} %get-tuple-element.634, s32[192]{0:T(256)S(1)} %select_reduce_fusion.3), kind=kLoop, calls=%fused_computation.32.clone.1 | loop fusion | flops 2686 | bytes 974 | tf_op jit(solution)/shard_map/while/body/eval_jaxpr/reduce_or | solution.py:110
  142.9 1.7 %conditional.5 = ((f32[2,8,96]{2,1,0:T(8,128)S(1)}, f32[2,8,96]{2,1,0:T(8,128)S(1)}, f32[2,8,96,128]{3,2,1,0:T(8,128)S(1)})) conditional(s32[]{:T(128)} %convert_element_type.67, (f32[2,8,96]{2,1,0:T(8,128)S(1)}, f32[2,8,96]{2,1,0:T(8,128)S(1)}, f32[2,8,96,128]{3,2,1,0:T(8,128)S(1)}) %tuple.74, (pred[192]{0:T(512)(128)(4,1)S(1)}, ...), branch_computations={%region_13.13_spmd, %region_14.16_spmd} | conditional | flops 154082304 | bytes 5875040 | solution.py:111
  145.3 1.7 %conditional.4 = ((f32[2,8,96]{2,1,0:T(8,128)S(1)}, f32[2,8,96]{2,1,0:T(8,128)S(1)}, f32[2,8,96,128]{3,2,1,0:T(8,128)S(1)})) conditional(s32[]{:T(128)} %convert_element_type.66, (f32[2,8,96]{2,1,0:T(8,128)S(1)}, f32[2,8,96]{2,1,0:T(8,128)S(1)}, f32[2,8,96,128]{3,2,1,0:T(8,128)S(1)}) %tuple.72, (pred[192]{0:T(512)(128)(4,1)S(1)}, s32[192]{0:T(256)S(1)}, ...), branch_computations={%region_8.8_spmd, %region_9.11_spmd} | conditional | flops 154082304 | bytes 5875040 | solution.py:111
  148.3 1.1 fusion.23
  (211 shorter events, 47.4 us)
Async XLA Ops:
  2.2 0.7 copy-start.3
  4.9 0.9 copy-start
  5.1 1.2 copy-start.4
  7.4 33.1 %copy-start.1 = (bf16[192,256]{1,0:T(8,128)(2,1)S(1)}, bf16[192,256]{1,0:T(8,128)(2,1)}, u32[]{:S(2)}) copy-start(bf16[192,256]{1,0:T(8,128)(2,1)} %param.14) | copy-start | bytes 294916
  72.5 1.3 copy-start.2
where the time goes:
time: 150 us; the launch traced here: 149 us
  blocking collectives  64 us (43%)
  other arithmetic  31.9 us (21%)
  matrix products  19.5 us (13%)
  local copies, waits for them, and re-layouts  17.1 us (11%)
  loops' own time  16.5 us (11%)
    all_gather x1, blocking collectives, local(): key_piece = lax.all_gather(k_ready, 'ctx', axis=0, tiled=True)  32.1 us
    all_gather x1, blocking collectives, local(): val_piece = lax.all_gather(values, 'ctx', axis=0, tiled=True)  32 us
    reduce_or x8, other arithmetic, step(): needed = jnp.any(key_live & (key_pos <= jnp.max(half_pos)))  15.6 us
    another operation x1, loops' own time, local(): lax.scan(step, (start_state, start_state), (key_blocks, val_blocks, jnp.a...  15.5 us
    dynamic_slice x32, local copies, waits for them, and re-layouts, local(): lax.scan(step, (start_state, start_state), (key_blocks, val_blocks, jnp.a...  13.4 us
    dot_general x16, matrix products, update(): jnp.einsum('kgqs,skd->kgqd', weights.astype(jnp.bfloat16), val_block, pre...  11.8 us
    dot_general x16, matrix products, update(): jnp.einsum('qkgd,skd->kgqs', query_half, key_block, preferred_element_typ...  7.62 us
    reduce_sum x16, other arithmetic, update(): new_total = old_total * rescale + jnp.sum(weights, -1)  5.31 us

commit v1 on v0

v1 whole, which is shorter than its diff:
```python
import functools
import math

import jax
import jax.numpy as jnp
import numpy as np
from jax import lax
from jax.experimental import pallas as pl
from jax.experimental.pallas import tpu as pltpu
from jax.sharding import PartitionSpec as P

MESH = pl.DeviceIdType.MESH
FAR = -1e30
THETA = 1000000.0
ROWS = 768


def rope_constants(shards, shard_rows, width):
    frequency = THETA ** (-np.arange(0, width, 2, dtype=np.float64) / width)
    frequency = np.concatenate([frequency, frequency])
    inner = np.arange(shard_rows)[:, None] * frequency[None, :]
    start = (np.arange(shards) * shard_rows)[:, None] * frequency[None, :]
    inner = np.stack([np.cos(inner), np.sin(inner)]).astype(np.float32)
    start = np.stack([np.cos(start), np.sin(start)], 1).astype(np.float32)
    return inner, start


def kernel(
    shards,
    width,
    q_in,
    k_in,
    v_in,
    q_gain,
    k_gain,
    counts,
    inner,
    start,
    out,
    kv,
    q_wide,
    top,
    total,
    summed,
    k_table,
    send_up,
    send_over,
    recv,
):
    shard_rows = q_in.shape[0]
    heads = q_in.shape[1] // width
    kv_heads = k_in.shape[1] // width
    group = heads // kv_heads
    pair_rows = 2 * shard_rows
    levels = shards // 2
    batch = max(1, min(group, ROWS // shard_rows))
    half = width // 2
    bf16, f32 = jnp.bfloat16, jnp.float32

    me = lax.axis_index("ctx")
    level = me // 2
    side = lax.rem(me, 2)
    over = me + 1 - 2 * side
    up = lax.rem(me + 2, shards)
    down = lax.rem(me - 2 + shards, shards)
    not_last = level < levels - 1
    not_first = level > 0

    barrier = pltpu.get_barrier_semaphore()
    pl.semaphore_signal(barrier, inc=1, device_id={"ctx": over}, device_id_type=MESH)

    @pl.when(not_last)
    def _():
        pl.semaphore_signal(barrier, inc=1, device_id={"ctx": up}, device_id_type=MESH)

    @pl.when(not_first)
    def _():
        pl.semaphore_signal(barrier, inc=1, device_id={"ctx": down}, device_id_type=MESH)

    def place(block, part):
        offset = pl.multiple_of(lax.rem(block, 2) * shard_rows, shard_rows)
        return kv.at[block // 2, part, pl.ds(offset, shard_rows), :]

    def copy(block, part, sems, target):
        return pltpu.make_async_remote_copy(
            src_ref=place(block, part),
            dst_ref=place(block, part),
            send_sem=sems.at[block, part],
            recv_sem=recv.at[block, part],
            device_id={"ctx": target},
            device_id_type=MESH,
        )

    def to_up(block, part):
        return copy(block, part, send_up, up)

    def to_over(block, part):
        return copy(block, part, send_over, over)

    c0 = start[me, 0:1, :]
    s0 = start[me, 1:2, :]
    ci = inner[0]
    si = inner[1]
    cosine = c0 * ci - s0 * si
    sine = s0 * ci + c0 * si
    lane = lax.broadcasted_iota(jnp.int32, (1, width), 1)
    sine = jnp.where(lane < half, -sine, sine)

    def tables(gain):
        g = gain[...]
        return cosine * g, sine * pltpu.roll(g, half, 1)

    def ready(x, by_cos, by_sin):
        x = x.astype(f32)
        scale = lax.rsqrt(jnp.mean(x * x, -1, keepdims=True) + 1e-06)
        return ((x * by_cos + pltpu.roll(x, half, 1) * by_sin) * scale).astype(bf16)

    live = lax.broadcasted_iota(jnp.int32, (shard_rows, width), 0) < counts[me]
    by_cos, by_sin = tables(k_gain)
    own = pl.multiple_of(side * shard_rows, shard_rows)
    for h in range(kv_heads):
        cut = slice(h * width, (h + 1) * width)
        k = ready(k_in[:, cut], by_cos, by_sin).astype(f32)
        k = jnp.where(live, k, k[0:1, :])
        kv[level, 0, pl.ds(own, shard_rows), cut] = k.astype(bf16)
        v = jnp.where(live, v_in[:, cut].astype(f32), 0.0)
        kv[level, 1, pl.ds(own, shard_rows), cut] = v.astype(bf16)

    @pl.when(side == 0)
    def _():
        for part in range(2):
            kv[level, part, shard_rows:, :] = jnp.zeros((shard_rows, kv_heads * width), bf16)

    pl.semaphore_wait(
        barrier, 1 + jnp.where(not_last, 1, 0) + jnp.where(not_first, 1, 0)
    )

    for part in range(2):

        @pl.when(side == 0)
        def _():
            to_over(me, part).start()

        @pl.when(not_last)
        def _():
            to_up(me, part).start()

    by_cos, by_sin = tables(q_gain)
    k_table[0] = by_cos
    k_table[1] = by_sin
    score_scale = math.log2(math.e) / math.sqrt(width)
    for h in range(heads):
        q = ready(q_in[:, h * width : (h + 1) * width], k_table[0], k_table[1])
        q = q.astype(f32) * score_scale
        high = q.astype(bf16)
        low = (q - high.astype(f32)).astype(bf16)
        q_wide[h, :, :width] = high
        q_wide[h, :, width:] = low

    @pl.when(side == 1)
    def _():
        to_over(me - 1, 0).wait_recv()

        @pl.when(not_last)
        def _():
            to_up(me - 1, 0).start()

    def relay(pair):
        block = 2 * pair + side
        for part in range(2):
            to_up(block, part).wait_recv()

            @pl.when(not_last)
            def _():
                to_up(block, part).start()

            if part == 0:

                @pl.when((side == 1) | (pair < level - 1))
                def _():
                    to_over(block, part).start()

            else:
                to_over(block, part).start()

    def attend(pair, first):
        blocks = [2 * pair, 2 * pair + 1]
        row = lax.broadcasted_iota(jnp.int32, (shard_rows, width), 0)
        alive = jnp.concatenate(
            [jnp.where(row < counts[b], 1.0, 0.0).astype(bf16) for b in blocks], 0
        )
        for h in range(kv_heads):
            cut = slice(h * width, (h + 1) * width)
            k = kv[pair, 0, :, cut]
            v = kv[pair, 1, :, cut]
            k2 = jnp.concatenate([k, k], 1)
            v2 = jnp.concatenate([v, alive], 1)

            @pl.loop(0, group // batch)
            def _(i):
                at = h * group + i * batch
                rows = batch * shard_rows
                q = q_wide[pl.ds(at, batch)].reshape(rows, 2 * width)
                s = lax.dot_general(
                    q, k2, (((1,), (1,)), ((), ())), preferred_element_type=f32
                )
                if first:
                    q_at = lax.broadcasted_iota(jnp.int32, (batch, shard_rows, pair_rows), 1)
                    k_at = lax.broadcasted_iota(jnp.int32, (batch, shard_rows, pair_rows), 2)
                    seen = (k_at <= q_at + side * shard_rows).reshape(rows, pair_rows)
                    s = jnp.where(seen, s, FAR)
                parts = [s[:, j : j + width] for j in range(0, pair_rows, width)]
                peak = functools.reduce(jnp.maximum, parts)
                peak = jnp.max(peak, -1, keepdims=True)
                state = pl.ds(pl.multiple_of(at * shard_rows, shard_rows), rows)
                if first:
                    new = jnp.broadcast_to(peak, (rows, width))
                else:
                    old = top[state, :]
                    new = jnp.maximum(old, peak)
                weights = jnp.concatenate(
                    [jnp.exp2(part - new).astype(bf16) for part in parts], 1
                )
                o = jnp.dot(weights, v2, preferred_element_type=f32)
                top[state, :] = new
                if first:
                    summed[state, :] = o[:, :width]
                    total[state, :] = o[:, width:]
                else:
                    rescale = jnp.exp2(old - new)
                    summed[state, :] = summed[state, :] * rescale + o[:, :width]
                    total[state, :] = total[state, :] * rescale + o[:, width:]

    def await_over(pair):
        block = 2 * pair + 1 - side
        for part in range(2):
            to_over(block, part).wait_recv()

    @pl.when(not_first)
    def _():
        relay(level - 1)

    @pl.when(side == 1)
    def _():
        to_over(me - 1, 1).wait_recv()

    attend(level, True)

    @pl.loop(0, level)
    def _(step):
        pair = level - 1 - step

        @pl.when(pair > 0)
        def _():
            relay(pair - 1)

        await_over(pair)
        attend(pair, False)

    for h in range(heads):
        state = slice(h * shard_rows, (h + 1) * shard_rows)
        o = summed[state, :] / total[state, :]
        out[:, h * width : (h + 1) * width] = jnp.where(live, o, 0.0).astype(bf16)

    for part in range(2):

        @pl.when(side == 0)
        def _():
            to_over(me, part).wait_send()

        @pl.when(not_last)
        def _():
            to_up(me, part).wait_send()

    @pl.when((side == 1) & not_last)
    def _():
        to_up(me - 1, 0).wait_send()

    @pl.loop(0, level)
    def _(pair):
        block = 2 * pair + side
        for part in range(2):

            @pl.when(not_last)
            def _():
                to_up(block, part).wait_send()

            if part == 0:

                @pl.when((side == 1) | (pair < level - 1))
                def _():
                    to_over(block, part).wait_send()

            else:
                to_over(block, part).wait_send()


def local(shards, queries, keys, values, q_gain, k_gain, counts):
    shard_rows = queries.shape[0]
    width = q_gain.shape[0]
    heads = queries.shape[1] // width
    inner, start = rope_constants(shards, shard_rows, width)
    vmem = pl.BlockSpec(memory_space=pltpu.VMEM)
    state = pltpu.VMEM((heads * shard_rows, width), jnp.float32)
    return pl.pallas_call(
        functools.partial(kernel, shards, width),
        out_shape=jax.ShapeDtypeStruct(queries.shape, jnp.bfloat16),
        in_specs=[vmem] * 5 + [pl.BlockSpec(memory_space=pltpu.SMEM)] + [vmem] * 2,
        out_specs=vmem,
        scratch_shapes=[
            pltpu.VMEM((shards // 2, 2, 2 * shard_rows, keys.shape[1]), jnp.bfloat16),
            pltpu.VMEM((heads, shard_rows, 2 * width), jnp.bfloat16),
            state,
            state,
            state,
            pltpu.VMEM((2, shard_rows, width), jnp.float32),
            pltpu.SemaphoreType.DMA((shards, 2)),
            pltpu.SemaphoreType.DMA((shards, 2)),
            pltpu.SemaphoreType.DMA((shards, 2)),
        ],
        compiler_params=pltpu.CompilerParams(
            collective_id=0, has_side_effects=True, vmem_limit_bytes=48 * 2**20
        ),
        name="attend",
    )(
        queries,
        keys,
        values,
        q_gain.reshape(1, width),
        k_gain.reshape(1, width),
        counts,
        jnp.asarray(inner),
        jnp.asarray(start),
    )


def solution(mesh):
    in_specs = (
        P(("groups", "ctx"), "tp"),
        P(("groups", "ctx"), "tp"),
        P(("groups", "ctx"), "tp"),
        P(),
        P(),
        P("groups"),
    )
    out_specs = P(("groups", "ctx"), "tp")
    return jax.shard_map(
        functools.partial(local, mesh.shape["ctx"]),
        mesh=mesh,
        in_specs=in_specs,
        out_specs=out_specs,
        check_vma=False,
    )
```

time: 150 us -> 33.6 us (0.22)
  the two profiles are of different devices: /device:TPU:28 before, /device:TPU:26 now
where the time goes in v1:
time: 33.6 us; the launch traced here: 33.3 us
  Pallas kernels  27.2 us (81%)
  local copies, waits for them, and re-layouts  6.1 us (18%)
    pallas_call x1, Pallas kernels, local(): pl.pallas_call(functools.partial(kernel, shards, width), out_shape=jax.Sh...  27.2 us
    unnamed x17, local copies, waits for them, and re-layouts  6.1 us

profile of v1, /device:TPU:26, one launch (start us, length us, event | category | flops | bytes accessed | tf_op | source)
XLA Modules:
  0.0 33.3 jit_solution(9648771100549904966)
XLA Ops:
  0.0 0.0 copy-start.5
  0.0 0.0 copy-start.6
  0.0 0.0 copy-start.7
  0.0 0.6 %copy-done.5 = f32[128]{0:T(128)S(1)} copy-done((f32[128]{0:T(128)S(1)}, f32[128]{0:T(128)}, u32[]{:S(2)}) %copy-start.5) | copy-done | bytes 536
  0.7 0.0 copy-done.6
  0.7 0.0 copy-done.7
  0.7 0.0 copy-start
  0.7 1.1 %copy-done = bf16[192,2048]{1,0:T(8,128)(2,1)S(1)} copy-done((bf16[192,2048]{1,0:T(8,128)(2,1)S(1)}, bf16[192,2048]{1,0:T(8,128)(2,1)}, u32[]{:S(2)}) %copy-start) | copy-done | bytes 786456
  1.8 0.0 copy-start.1
  1.8 0.9 %copy-done.1 = f32[2,192,128]{2,1,0:T(8,128)S(1)} copy-done((f32[2,192,128]{2,1,0:T(8,128)S(1)}, f32[2,192,128]{2,1,0:T(8,128)}, u32[]{:S(2)}) %copy-start.1) | copy-done | bytes 196632
  2.7 0.0 copy-start.2
  2.8 0.9 %copy-done.2 = bf16[192,256]{1,0:T(8,128)(2,1)S(1)} copy-done((bf16[192,256]{1,0:T(8,128)(2,1)S(1)}, bf16[192,256]{1,0:T(8,128)(2,1)}, u32[]{:S(2)}) %copy-start.2) | copy-done | bytes 98328
  3.6 0.0 copy-start.3
  3.6 0.9 %copy-done.3 = bf16[192,256]{1,0:T(8,128)(2,1)S(1)} copy-done((bf16[192,256]{1,0:T(8,128)(2,1)S(1)}, bf16[192,256]{1,0:T(8,128)(2,1)}, u32[]{:S(2)}) %copy-start.3) | copy-done | bytes 98328
  4.5 0.0 copy-start.4
  4.5 0.7 %copy-done.4 = f32[8,2,128]{2,1,0:T(2,128)S(1)} copy-done((f32[8,2,128]{2,1,0:T(2,128)S(1)}, f32[8,2,128]{2,1,0:T(2,128)}, u32[]{:S(2)}) %copy-start.4) | copy-done | bytes 8216
  5.2 27.2 %attend.1 = bf16[192,2048]{1,0:T(8,128)(2,1)S(1)} custom-call(bf16[192,2048]{1,0:T(8,128)(2,1)S(1)} %copy-done, bf16[192,256]{1,0:T(8,128)(2,1)S(1)} %copy-done.2, bf16[192,256]{1,0:T(8,128)(2,1)S(1)} %copy-done.3, f32[1,128]{1,0:T(1,128)S(1)} %bitcast.2, f32[1,128]{1,0:T(1,128)S(1)} %bitcast.3, s32[8]{0:T(128)S(1)} %copy-done.7, ...), custom_call_target="tpu_custom_call" | custom-call | tf_op jit(solution)/shard_map/attend/pallas_call | solution.py:305
  32.4 0.9 %copy.10 = bf16[192,2048]{1,0:T(8,128)(2,1)} copy(bf16[192,2048]{1,0:T(8,128)(2,1)S(1)} %attend.1) | data formatting | bytes 1572864
Async XLA Ops:
  0.0 0.7 %copy-start.5 = (f32[128]{0:T(128)S(1)}, f32[128]{0:T(128)}, u32[]{:S(2)}) copy-start(f32[128]{0:T(128)} %param.11) | copy-start | bytes 1540
  0.0 0.7 %copy-start.6 = (f32[128]{0:T(128)S(1)}, f32[128]{0:T(128)}, u32[]{:S(2)}) copy-start(f32[128]{0:T(128)} %param.12) | copy-start | bytes 1540
  0.0 0.7 %copy-start.7 = (s32[8]{0:T(128)S(1)}, s32[8]{0:T(128)}, u32[]{:S(2)}) copy-start(s32[8]{0:T(128)} %counts.1) | copy-start | bytes 100
  0.7 1.1 %copy-start = (bf16[192,2048]{1,0:T(8,128)(2,1)S(1)}, bf16[192,2048]{1,0:T(8,128)(2,1)}, u32[]{:S(2)}) copy-start(bf16[192,2048]{1,0:T(8,128)(2,1)} %q_in.1) | copy-start | bytes 2359300
  1.8 0.9 %copy-start.1 = (f32[2,192,128]{2,1,0:T(8,128)S(1)}, f32[2,192,128]{2,1,0:T(8,128)}, u32[]{:S(2)}) copy-start(f32[2,192,128]{2,1,0:T(8,128)} %constant.4.clone.inner) | copy-start | bytes 589828
  2.7 0.9 %copy-start.2 = (bf16[192,256]{1,0:T(8,128)(2,1)S(1)}, bf16[192,256]{1,0:T(8,128)(2,1)}, u32[]{:S(2)}) copy-start(bf16[192,256]{1,0:T(8,128)(2,1)} %k_in.1) | copy-start | bytes 294916
  3.6 0.9 %copy-start.3 = (bf16[192,256]{1,0:T(8,128)(2,1)S(1)}, bf16[192,256]{1,0:T(8,128)(2,1)}, u32[]{:S(2)}) copy-start(bf16[192,256]{1,0:T(8,128)(2,1)} %v_in.1) | copy-start | bytes 294916
  4.5 0.7 %copy-start.4 = (f32[8,2,128]{2,1,0:T(2,128)S(1)}, f32[8,2,128]{2,1,0:T(2,128)}, u32[]{:S(2)}) copy-start(f32[8,2,128]{2,1,0:T(2,128)} %constant.5.clone.start) | copy-start | bytes 24580

commit v2 on v1

--- a/solution.py
+++ b/solution.py
@@ -12,7 +12,7 @@
 MESH = pl.DeviceIdType.MESH
 FAR = -1e30
 THETA = 1000000.0
-ROWS = 768
+ROWS = 384
 
 
 def rope_constants(shards, shard_rows, width):
@@ -28,15 +28,22 @@
 def kernel(
     shards,
     width,
+    q_hbm,
+    k_hbm,
+    v_hbm,
+    q_gain_hbm,
+    k_gain_hbm,
+    counts,
+    inner_hbm,
+    start_hbm,
+    out,
     q_in,
     k_in,
     v_in,
     q_gain,
     k_gain,
-    counts,
     inner,
     start,
-    out,
     kv,
     q_wide,
     top,
@@ -46,6 +53,7 @@
     send_up,
     send_over,
     recv,
+    fetched,
 ):
     shard_rows = q_in.shape[0]
     heads = q_in.shape[1] // width
@@ -66,6 +74,23 @@
     not_last = level < levels - 1
     not_first = level > 0
 
+    fetches = [
+        pltpu.make_async_copy(source, target, fetched.at[i])
+        for i, (source, target) in enumerate(
+            [
+                (k_hbm, k_in),
+                (inner_hbm, inner),
+                (start_hbm.at[me], start),
+                (k_gain_hbm, k_gain),
+                (v_hbm, v_in),
+                (q_gain_hbm, q_gain),
+                (q_hbm, q_in),
+            ]
+        )
+    ]
+    for fetch in fetches:
+        fetch.start()
+
     barrier = pltpu.get_barrier_semaphore()
     pl.semaphore_signal(barrier, inc=1, device_id={"ctx": over}, device_id_type=MESH)
 
@@ -97,8 +122,10 @@
     def to_over(block, part):
         return copy(block, part, send_over, over)
 
-    c0 = start[me, 0:1, :]
-    s0 = start[me, 1:2, :]
+    for fetch in fetches[:5]:
+        fetch.wait()
+    c0 = start[0:1, :]
+    s0 = start[1:2, :]
     ci = inner[0]
     si = inner[1]
     cosine = c0 * ci - s0 * si
@@ -145,6 +172,8 @@
         def _():
             to_up(me, part).start()
 
+    for fetch in fetches[5:]:
+        fetch.wait()
     by_cos, by_sin = tables(q_gain)
     k_table[0] = by_cos
     k_table[1] = by_sin
@@ -154,16 +183,9 @@
         q = q.astype(f32) * score_scale
         high = q.astype(bf16)
         low = (q - high.astype(f32)).astype(bf16)
-        q_wide[h, :, :width] = high
-        q_wide[h, :, width:] = low
-
-    @pl.when(side == 1)
-    def _():
-        to_over(me - 1, 0).wait_recv()
-
-        @pl.when(not_last)
-        def _():
-            to_up(me - 1, 0).start()
+        at = (h % group) * shard_rows
+        q_wide[h // group, at : at + shard_rows, :width] = high
+        q_wide[h // group, at : at + shard_rows, width:] = low
 
     def relay(pair):
         block = 2 * pair + side
@@ -176,12 +198,27 @@
 
             if part == 0:
 
-                @pl.when((side == 1) | (pair < level - 1))
+                @pl.when((side == 1) | (pair > 0))
                 def _():
                     to_over(block, part).start()
 
             else:
                 to_over(block, part).start()
+
+    def detour():
+        @pl.when(side == 1)
+        def _():
+            @pl.when(not_first)
+            def _():
+                to_up(0, 0).wait_recv()
+
+            @pl.when(level == 0)
+            def _():
+                to_over(0, 0).wait_recv()
+
+            @pl.when(not_last)
+            def _():
+                to_up(0, 0).start()
 
     def attend(pair, first):
         blocks = [2 * pair, 2 * pair + 1]
@@ -189,59 +226,80 @@
         alive = jnp.concatenate(
             [jnp.where(row < counts[b], 1.0, 0.0).astype(bf16) for b in blocks], 0
         )
-        for h in range(kv_heads):
-            cut = slice(h * width, (h + 1) * width)
+        if first:
+            q_at = lax.broadcasted_iota(jnp.int32, (shard_rows, pair_rows), 0)
+            k_at = lax.broadcasted_iota(jnp.int32, (shard_rows, pair_rows), 1)
+            seen = k_at <= q_at + side * shard_rows
+            seen = jnp.concatenate([seen] * batch, 0) if batch > 1 else seen
+
+        @pl.loop(0, kv_heads)
+        def _(h):
+            cut = pl.ds(pl.multiple_of(h * width, width), width)
             k = kv[pair, 0, :, cut]
             v = kv[pair, 1, :, cut]
             k2 = jnp.concatenate([k, k], 1)
             v2 = jnp.concatenate([v, alive], 1)
-
-            @pl.loop(0, group // batch)
-            def _(i):
-                at = h * group + i * batch
-                rows = batch * shard_rows
-                q = q_wide[pl.ds(at, batch)].reshape(rows, 2 * width)
-                s = lax.dot_general(
+            rows = batch * shard_rows
+
+            def scores(i):
+                q = q_wide[h, pl.ds(i * rows, rows), :]
+                return lax.dot_general(
                     q, k2, (((1,), (1,)), ((), ())), preferred_element_type=f32
                 )
+
+            steps = group // batch
+            coming = scores(0)
+            for i in range(steps):
+                s = coming
+                if i + 1 < steps:
+                    coming = scores(i + 1)
                 if first:
-                    q_at = lax.broadcasted_iota(jnp.int32, (batch, shard_rows, pair_rows), 1)
-                    k_at = lax.broadcasted_iota(jnp.int32, (batch, shard_rows, pair_rows), 2)
-                    seen = (k_at <= q_at + side * shard_rows).reshape(rows, pair_rows)
                     s = jnp.where(seen, s, FAR)
                 parts = [s[:, j : j + width] for j in range(0, pair_rows, width)]
                 peak = functools.reduce(jnp.maximum, parts)
                 peak = jnp.max(peak, -1, keepdims=True)
-                state = pl.ds(pl.multiple_of(at * shard_rows, shard_rows), rows)
+                state = (h, slice(i * rows, (i + 1) * rows))
                 if first:
                     new = jnp.broadcast_to(peak, (rows, width))
                 else:
-                    old = top[state, :]
+                    old = top[state]
                     new = jnp.maximum(old, peak)
                 weights = jnp.concatenate(
                     [jnp.exp2(part - new).astype(bf16) for part in parts], 1
                 )
                 o = jnp.dot(weights, v2, preferred_element_type=f32)
-                top[state, :] = new
+                top[state] = new
                 if first:
-                    summed[state, :] = o[:, :width]
-                    total[state, :] = o[:, width:]
+                    summed[state] = o[:, :width]
+                    total[state] = o[:, width:]
                 else:
                     rescale = jnp.exp2(old - new)
-                    summed[state, :] = summed[state, :] * rescale + o[:, :width]
-                    total[state, :] = total[state, :] * rescale + o[:, width:]
+                    summed[state] = summed[state] * rescale + o[:, :width]
+                    total[state] = total[state] * rescale + o[:, width:]
 
     def await_over(pair):
         block = 2 * pair + 1 - side
-        for part in range(2):
-            to_over(block, part).wait_recv()
+
+        @pl.when((side == 0) | (pair > 0))
+        def _():
+            to_over(block, 0).wait_recv()
+
+        to_over(block, 1).wait_recv()
 
     @pl.when(not_first)
     def _():
         relay(level - 1)
 
+    @pl.when(level == 0)
+    def _():
+        detour()
+
     @pl.when(side == 1)
     def _():
+        @pl.when(not_first)
+        def _():
+            to_over(me - 1, 0).wait_recv()
+
         to_over(me - 1, 1).wait_recv()
 
     attend(level, True)
@@ -254,12 +312,17 @@
         def _():
             relay(pair - 1)
 
+        @pl.when(pair == 0)
+        def _():
+            detour()
+
         await_over(pair)
         attend(pair, False)
 
     for h in range(heads):
-        state = slice(h * shard_rows, (h + 1) * shard_rows)
-        o = summed[state, :] / total[state, :]
+        at = (h % group) * shard_rows
+        state = (h // group, slice(at, at + shard_rows))
+        o = summed[state] / total[state]
         out[:, h * width : (h + 1) * width] = jnp.where(live, o, 0.0).astype(bf16)
 
     for part in range(2):
@@ -274,7 +337,7 @@
 
     @pl.when((side == 1) & not_last)
     def _():
-        to_up(me - 1, 0).wait_send()
+        to_up(0, 0).wait_send()
 
     @pl.loop(0, level)
     def _(pair):
@@ -287,7 +350,7 @@
 
             if part == 0:
 
-                @pl.when((side == 1) | (pair < level - 1))
+                @pl.when((side == 1) | (pair > 0))
                 def _():
                     to_over(block, part).wait_send()
 
@@ -301,15 +364,25 @@
     heads = queries.shape[1] // width
     inner, start = rope_constants(shards, shard_rows, width)
     vmem = pl.BlockSpec(memory_space=pltpu.VMEM)
-    state = pltpu.VMEM((heads * shard_rows, width), jnp.float32)
+    hbm = pl.BlockSpec(memory_space=pl.ANY)
+    kv_heads = keys.shape[1] // width
+    rows = heads // kv_heads * shard_rows
+    state = pltpu.VMEM((kv_heads, rows, width), jnp.float32)
     return pl.pallas_call(
         functools.partial(kernel, shards, width),
         out_shape=jax.ShapeDtypeStruct(queries.shape, jnp.bfloat16),
-        in_specs=[vmem] * 5 + [pl.BlockSpec(memory_space=pltpu.SMEM)] + [vmem] * 2,
+        in_specs=[hbm] * 5 + [pl.BlockSpec(memory_space=pltpu.SMEM)] + [hbm] * 2,
         out_specs=vmem,
         scratch_shapes=[
+            pltpu.VMEM(queries.shape, jnp.bfloat16),
+            pltpu.VMEM(keys.shape, jnp.bfloat16),
+            pltpu.VMEM(values.shape, jnp.bfloat16),
+            pltpu.VMEM((1, width), jnp.float32),
+            pltpu.VMEM((1, width), jnp.float32),
+            pltpu.VMEM(inner.shape, jnp.float32),
+            pltpu.VMEM(start.shape[1:], jnp.float32),
             pltpu.VMEM((shards // 2, 2, 2 * shard_rows, keys.shape[1]), jnp.bfloat16),
-            pltpu.VMEM((heads, shard_rows, 2 * width), jnp.bfloat16),
+            pltpu.VMEM((kv_heads, rows, 2 * width), jnp.bfloat16),
             state,
             state,
             state,
@@ -317,9 +390,10 @@
             pltpu.SemaphoreType.DMA((shards, 2)),
             pltpu.SemaphoreType.DMA((shards, 2)),
             pltpu.SemaphoreType.DMA((shards, 2)),
+            pltpu.SemaphoreType.DMA((7,)),
         ],
         compiler_params=pltpu.CompilerParams(
-            collective_id=0, has_side_effects=True, vmem_limit_bytes=48 * 2**20
+            collective_id=0, has_side_effects=True, vmem_limit_bytes=60 * 2**20
         ),
         name="attend",
     )(

time: 33.6 us -> 27.3 us (0.81)
  local copies, waits for them, and re-layouts: 6.1 us -> 2.09 us
  Pallas kernels: 27.2 us -> 25 us
    unnamed x17 -> x1, local copies, waits for them, and re-layouts: 6.1 us -> 2.09 us
    pallas_call x1, Pallas kernels: 27.2 us -> 25 us  [local(): pl.pallas_call(functools.partial(kernel, shards, width), out_shape=jax.Sh...]
where the time goes in v2:
time: 27.3 us; the launch traced here: 27.1 us
  Pallas kernels  25 us (92%)
  local copies, waits for them, and re-layouts  2.09 us (8%)
    pallas_call x1, Pallas kernels, local(): pl.pallas_call(functools.partial(kernel, shards, width), out_shape=jax.Sh...  25 us
    unnamed x1, local copies, waits for them, and re-layouts  2.09 us

profile of v2, /device:TPU:26, one launch (start us, length us, event | category | flops | bytes accessed | tf_op | source)
XLA Modules:
  0.0 27.1 jit_solution(7952785557403811699)
XLA Ops:
  0.0 25.0 %attend.1 = bf16[192,2048]{1,0:T(8,128)(2,1)} custom-call(bf16[192,2048]{1,0:T(8,128)(2,1)} %q_hbm.1, bf16[192,256]{1,0:T(8,128)(2,1)} %k_hbm.1, bf16[192,256]{1,0:T(8,128)(2,1)} %v_hbm.1, f32[1,128]{1,0:T(1,128)} %bitcast.2, f32[1,128]{1,0:T(1,128)} %bitcast.3, s32[8]{0:T(128)} %counts.1, f32[2,192,128]{2,1,0:T(8,128)} %constant.4.clone.inner_hbm, ...), custom_call_target="tpu_custom_call" | custom-call | tf_op jit(solution)/shard_map/attend/pallas_call | solution.py:371
  25.0 2.1 %copy.10 = bf16[192,2048]{1,0:T(8,128)(2,1)} copy(bf16[192,2048]{1,0:T(8,128)(2,1)} %attend.1) | data formatting | bytes 1572864

commit v3 on v2

--- a/solution.py
+++ b/solution.py
@@ -9,6 +9,7 @@
 from jax.experimental.pallas import tpu as pltpu
 from jax.sharding import PartitionSpec as P
 
+KEYS, VALUES = 0, 1
 MESH = pl.DeviceIdType.MESH
 FAR = -1e30
 THETA = 1000000.0
@@ -33,15 +34,15 @@
     v_hbm,
     q_gain_hbm,
     k_gain_hbm,
-    counts,
+    counts_hbm,
     inner_hbm,
     start_hbm,
     out,
     q_in,
     k_in,
-    v_in,
     q_gain,
     k_gain,
+    counts,
     inner,
     start,
     kv,
@@ -54,6 +55,8 @@
     send_over,
     recv,
     fetched,
+    result,
+    leaving,
 ):
     shard_rows = q_in.shape[0]
     heads = q_in.shape[1] // width
@@ -73,6 +76,7 @@
     down = lax.rem(me - 2 + shards, shards)
     not_last = level < levels - 1
     not_first = level > 0
+    own = pl.multiple_of(side * shard_rows, shard_rows)
 
     fetches = [
         pltpu.make_async_copy(source, target, fetched.at[i])
@@ -82,9 +86,10 @@
                 (inner_hbm, inner),
                 (start_hbm.at[me], start),
                 (k_gain_hbm, k_gain),
-                (v_hbm, v_in),
+                (counts_hbm, counts),
                 (q_gain_hbm, q_gain),
                 (q_hbm, q_in),
+                (v_hbm, kv.at[level, VALUES, pl.ds(own, shard_rows), :]),
             ]
         )
     ]
@@ -106,9 +111,9 @@
         offset = pl.multiple_of(lax.rem(block, 2) * shard_rows, shard_rows)
         return kv.at[block // 2, part, pl.ds(offset, shard_rows), :]
 
-    def copy(block, part, sems, target):
+    def copy(block, part, sems, target, source):
         return pltpu.make_async_remote_copy(
-            src_ref=place(block, part),
+            src_ref=place(block, part) if source is None else source,
             dst_ref=place(block, part),
             send_sem=sems.at[block, part],
             recv_sem=recv.at[block, part],
@@ -116,11 +121,32 @@
             device_id_type=MESH,
         )
 
-    def to_up(block, part):
-        return copy(block, part, send_up, up)
-
-    def to_over(block, part):
-        return copy(block, part, send_over, over)
+    def to_up(block, part, source=None):
+        return copy(block, part, send_up, up, source)
+
+    def to_over(block, part, source=None):
+        return copy(block, part, send_over, over, source)
+
+    pl.semaphore_wait(
+        barrier, 1 + jnp.where(not_last, 1, 0) + jnp.where(not_first, 1, 0)
+    )
+
+    @pl.when(side == 0)
+    def _():
+        to_over(me, VALUES, v_hbm).start()
+
+    @pl.when(not_last)
+    def _():
+        to_up(me, VALUES, v_hbm).start()
+
+    def send_own_keys():
+        @pl.when((side == 0) | (level == 0))
+        def _():
+            to_over(me, KEYS).start()
+
+        @pl.when(not_last)
+        def _():
+            to_up(me, KEYS).start()
 
     for fetch in fetches[:5]:
         fetch.wait()
@@ -144,41 +170,30 @@
 
     live = lax.broadcasted_iota(jnp.int32, (shard_rows, width), 0) < counts[me]
     by_cos, by_sin = tables(k_gain)
-    own = pl.multiple_of(side * shard_rows, shard_rows)
     for h in range(kv_heads):
         cut = slice(h * width, (h + 1) * width)
         k = ready(k_in[:, cut], by_cos, by_sin).astype(f32)
         k = jnp.where(live, k, k[0:1, :])
-        kv[level, 0, pl.ds(own, shard_rows), cut] = k.astype(bf16)
-        v = jnp.where(live, v_in[:, cut].astype(f32), 0.0)
-        kv[level, 1, pl.ds(own, shard_rows), cut] = v.astype(bf16)
+        kv[level, KEYS, pl.ds(own, shard_rows), cut] = k.astype(bf16)
 
     @pl.when(side == 0)
     def _():
-        for part in range(2):
-            kv[level, part, shard_rows:, :] = jnp.zeros((shard_rows, kv_heads * width), bf16)
-
-    pl.semaphore_wait(
-        barrier, 1 + jnp.where(not_last, 1, 0) + jnp.where(not_first, 1, 0)
-    )
-
-    for part in range(2):
-
-        @pl.when(side == 0)
-        def _():
-            to_over(me, part).start()
-
-        @pl.when(not_last)
-        def _():
-            to_up(me, part).start()
-
-    for fetch in fetches[5:]:
+        blank = jnp.zeros((shard_rows, kv_heads * width), bf16)
+        kv[level, VALUES, shard_rows:, :] = blank
+
+        @pl.when(not_first)
+        def _():
+            kv[level, KEYS, shard_rows:, :] = blank
+
+    for fetch in fetches[5:7]:
         fetch.wait()
     by_cos, by_sin = tables(q_gain)
     k_table[0] = by_cos
     k_table[1] = by_sin
     score_scale = math.log2(math.e) / math.sqrt(width)
     for h in range(heads):
+        if h == 0:
+            send_own_keys()
         q = ready(q_in[:, h * width : (h + 1) * width], k_table[0], k_table[1])
         q = q.astype(f32) * score_scale
         high = q.astype(bf16)
@@ -189,38 +204,56 @@
 
     def relay(pair):
         block = 2 * pair + side
-        for part in range(2):
-            to_up(block, part).wait_recv()
-
-            @pl.when(not_last)
-            def _():
-                to_up(block, part).start()
-
-            if part == 0:
-
-                @pl.when((side == 1) | (pair > 0))
-                def _():
-                    to_over(block, part).start()
-
-            else:
-                to_over(block, part).start()
+
+        to_up(block, VALUES).wait_recv()
+
+        @pl.when(not_last)
+        def _():
+            to_up(block, VALUES).start()
+
+        to_over(block, VALUES).start()
+
+        to_up(block, KEYS).wait_recv()
+
+        @pl.when(not_last)
+        def _():
+            to_up(block, KEYS).start()
+
+        @pl.when(pair > 0)
+        def _():
+            to_over(block, KEYS).start()
 
     def detour():
-        @pl.when(side == 1)
-        def _():
-            @pl.when(not_first)
-            def _():
-                to_up(0, 0).wait_recv()
-
-            @pl.when(level == 0)
-            def _():
-                to_over(0, 0).wait_recv()
-
-            @pl.when(not_last)
-            def _():
-                to_up(0, 0).start()
-
-    def attend(pair, first):
+        @pl.when(not_first)
+        def _():
+            to_up(1 - side, KEYS).wait_recv()
+
+        @pl.when(level == 0)
+        def _():
+            to_over(1 - side, KEYS).wait_recv()
+
+        @pl.when(not_last)
+        def _():
+            to_up(side, KEYS).wait_send()
+            to_up(1 - side, KEYS).start()
+
+    def finish(h, i, o):
+        row = lax.broadcasted_iota(jnp.int32, (shard_rows, width), 0)
+        for n in range(batch):
+            done = o[n * shard_rows : (n + 1) * shard_rows]
+            done = jnp.where(row < counts[me], done, 0.0).astype(bf16)
+            done_at = slice((i * batch + n) * width, (i * batch + n + 1) * width)
+            result[h, :, done_at] = done
+
+    def leave(h):
+        part = group * width
+        return pltpu.make_async_copy(
+            result.at[h],
+            out.at[:, pl.ds(pl.multiple_of(h * part, part), part)],
+            leaving.at[h],
+        )
+
+    def attend(pair, first, last=False):
         blocks = [2 * pair, 2 * pair + 1]
         row = lax.broadcasted_iota(jnp.int32, (shard_rows, width), 0)
         alive = jnp.concatenate(
@@ -235,8 +268,8 @@
         @pl.loop(0, kv_heads)
         def _(h):
             cut = pl.ds(pl.multiple_of(h * width, width), width)
-            k = kv[pair, 0, :, cut]
-            v = kv[pair, 1, :, cut]
+            k = kv[pair, KEYS, :, cut]
+            v = kv[pair, VALUES, :, cut] * alive
             k2 = jnp.concatenate([k, k], 1)
             v2 = jnp.concatenate([v, alive], 1)
             rows = batch * shard_rows
@@ -268,6 +301,12 @@
                     [jnp.exp2(part - new).astype(bf16) for part in parts], 1
                 )
                 o = jnp.dot(weights, v2, preferred_element_type=f32)
+                if last:
+                    rescale = jnp.exp2(old - new)
+                    over_total = 1.0 / (total[state] * rescale + o[:, width:])
+                    o = (summed[state] * rescale + o[:, :width]) * over_total
+                    finish(h, i, o)
+                    continue
                 top[state] = new
                 if first:
                     summed[state] = o[:, :width]
@@ -277,14 +316,17 @@
                     summed[state] = summed[state] * rescale + o[:, :width]
                     total[state] = total[state] * rescale + o[:, width:]
 
+            if last:
+                leave(h).start()
+
     def await_over(pair):
         block = 2 * pair + 1 - side
 
-        @pl.when((side == 0) | (pair > 0))
-        def _():
-            to_over(block, 0).wait_recv()
-
-        to_over(block, 1).wait_recv()
+        @pl.when(pair > 0)
+        def _():
+            to_over(block, KEYS).wait_recv()
+
+        to_over(block, VALUES).wait_recv()
 
     @pl.when(not_first)
     def _():
@@ -298,64 +340,71 @@
     def _():
         @pl.when(not_first)
         def _():
-            to_over(me - 1, 0).wait_recv()
-
-        to_over(me - 1, 1).wait_recv()
-
+            to_over(me - 1, KEYS).wait_recv()
+
+        to_over(me - 1, VALUES).wait_recv()
+
+    fetches[7].wait()
     attend(level, True)
 
-    @pl.loop(0, level)
+    @pl.loop(0, level - 1)
     def _(step):
         pair = level - 1 - step
-
-        @pl.when(pair > 0)
-        def _():
-            relay(pair - 1)
-
-        @pl.when(pair == 0)
-        def _():
-            detour()
-
+        relay(pair - 1)
         await_over(pair)
         attend(pair, False)
 
-    for h in range(heads):
-        at = (h % group) * shard_rows
-        state = (h // group, slice(at, at + shard_rows))
-        o = summed[state] / total[state]
-        out[:, h * width : (h + 1) * width] = jnp.where(live, o, 0.0).astype(bf16)
-
-    for part in range(2):
-
-        @pl.when(side == 0)
-        def _():
-            to_over(me, part).wait_send()
-
-        @pl.when(not_last)
-        def _():
-            to_up(me, part).wait_send()
-
-    @pl.when((side == 1) & not_last)
-    def _():
-        to_up(0, 0).wait_send()
+    @pl.when(not_first)
+    def _():
+        detour()
+        await_over(0)
+        attend(0, False, True)
+
+    @pl.when(level == 0)
+    def _():
+        @pl.loop(0, kv_heads)
+        def _(h):
+            for i in range(group // batch):
+                state = (h, slice(i * batch * shard_rows, (i + 1) * batch * shard_rows))
+                finish(h, i, summed[state] * (1.0 / total[state]))
+            leave(h).start()
+
+    for h in range(kv_heads):
+        leave(h).wait()
+
+    @pl.when(side == 0)
+    def _():
+        to_over(me, VALUES).wait_send()
+
+    @pl.when((side == 0) | (level == 0))
+    def _():
+        to_over(me, KEYS).wait_send()
+
+    @pl.when(not_last)
+    def _():
+        to_up(me, VALUES).wait_send()
+        to_up(1 - side, KEYS).wait_send()
+
+        @pl.when(not_first)
+        def _():
+            to_up(me, KEYS).wait_send()
 
     @pl.loop(0, level)
     def _(pair):
         block = 2 * pair + side
-        for part in range(2):
-
-            @pl.when(not_last)
+        to_over(block, VALUES).wait_send()
+
+        @pl.when(pair > 0)
+        def _():
+            to_over(block, KEYS).wait_send()
+
+        @pl.when(not_last)
+        def _():
+            to_up(block, VALUES).wait_send()
+
+            @pl.when(pair > 0)
             def _():
-                to_up(block, part).wait_send()
-
-            if part == 0:
-
-                @pl.when((side == 1) | (pair > 0))
-                def _():
-                    to_over(block, part).wait_send()
-
-            else:
-                to_over(block, part).wait_send()
+                to_up(block, KEYS).wait_send()
 
 
 def local(shards, queries, keys, values, q_gain, k_gain, counts):
@@ -363,7 +412,6 @@
     width = q_gain.shape[0]
     heads = queries.shape[1] // width
     inner, start = rope_constants(shards, shard_rows, width)
-    vmem = pl.BlockSpec(memory_space=pltpu.VMEM)
     hbm = pl.BlockSpec(memory_space=pl.ANY)
     kv_heads = keys.shape[1] // width
     rows = heads // kv_heads * shard_rows
@@ -371,14 +419,14 @@
     return pl.pallas_call(
         functools.partial(kernel, shards, width),
         out_shape=jax.ShapeDtypeStruct(queries.shape, jnp.bfloat16),
-        in_specs=[hbm] * 5 + [pl.BlockSpec(memory_space=pltpu.SMEM)] + [hbm] * 2,
-        out_specs=vmem,
+        in_specs=[hbm] * 8,
+        out_specs=hbm,
         scratch_shapes=[
             pltpu.VMEM(queries.shape, jnp.bfloat16),
             pltpu.VMEM(keys.shape, jnp.bfloat16),
-            pltpu.VMEM(values.shape, jnp.bfloat16),
             pltpu.VMEM((1, width), jnp.float32),
             pltpu.VMEM((1, width), jnp.float32),
+            pltpu.SMEM(counts.shape, jnp.int32),
             pltpu.VMEM(inner.shape, jnp.float32),
             pltpu.VMEM(start.shape[1:], jnp.float32),
             pltpu.VMEM((shards // 2, 2, 2 * shard_rows, keys.shape[1]), jnp.bfloat16),
@@ -390,7 +438,9 @@
             pltpu.SemaphoreType.DMA((shards, 2)),
             pltpu.SemaphoreType.DMA((shards, 2)),
             pltpu.SemaphoreType.DMA((shards, 2)),
-            pltpu.SemaphoreType.DMA((7,)),
+            pltpu.SemaphoreType.DMA((8,)),
+            pltpu.VMEM((kv_heads, shard_rows, queries.shape[1] // kv_heads), jnp.bfloat16),
+            pltpu.SemaphoreType.DMA((kv_heads,)),
         ],
         compiler_params=pltpu.CompilerParams(
             collective_id=0, has_side_effects=True, vmem_limit_bytes=60 * 2**20

time: 27.3 us -> 25.4 us (0.930)
  Pallas kernels: 25 us -> 23.2 us
    pallas_call x1, Pallas kernels: 25 us -> 23.2 us  [local(): pl.pallas_call(functools.partial(kernel, shards, width), out_shape=jax.Sh...]
where the time goes in v3:
time: 25.4 us; the launch traced here: 25.3 us
  Pallas kernels  23.2 us (91%)
  local copies, waits for them, and re-layouts  2.09 us (8%)
    pallas_call x1, Pallas kernels, local(): pl.pallas_call(functools.partial(kernel, shards, width), out_shape=jax.Sh...  23.2 us
    unnamed x1, local copies, waits for them, and re-layouts  2.09 us

profile of v3, /device:TPU:26, one launch (start us, length us, event | category | flops | bytes accessed | tf_op | source)
XLA Modules:
  0.0 25.3 jit_solution(18180548477859931396)
XLA Ops:
  0.0 23.2 %attend.1 = bf16[192,2048]{1,0:T(8,128)(2,1)} custom-call(bf16[192,2048]{1,0:T(8,128)(2,1)} %q_hbm.1, bf16[192,256]{1,0:T(8,128)(2,1)} %k_hbm.1, bf16[192,256]{1,0:T(8,128)(2,1)} %v_hbm.1, f32[1,128]{1,0:T(1,128)} %bitcast.2, f32[1,128]{1,0:T(1,128)} %bitcast.3, s32[8]{0:T(128)} %counts_hbm.1, f32[2,192,128]{2,1,0:T(8,128)} %constant.4.clone.inner_hbm, ...), custom_call_target="tpu_custom_call" | custom-call | tf_op jit(solution)/shard_map/attend/pallas_call | solution.py:419
  23.2 2.1 %copy.10 = bf16[192,2048]{1,0:T(8,128)(2,1)} copy(bf16[192,2048]{1,0:T(8,128)(2,1)} %attend.1) | data formatting | bytes 1572864

commit v4 on v3

--- a/solution.py
+++ b/solution.py
@@ -55,8 +55,6 @@
     send_over,
     recv,
     fetched,
-    result,
-    leaving,
 ):
     shard_rows = q_in.shape[0]
     heads = q_in.shape[1] // width
@@ -242,16 +240,8 @@
         for n in range(batch):
             done = o[n * shard_rows : (n + 1) * shard_rows]
             done = jnp.where(row < counts[me], done, 0.0).astype(bf16)
-            done_at = slice((i * batch + n) * width, (i * batch + n + 1) * width)
-            result[h, :, done_at] = done
-
-    def leave(h):
-        part = group * width
-        return pltpu.make_async_copy(
-            result.at[h],
-            out.at[:, pl.ds(pl.multiple_of(h * part, part), part)],
-            leaving.at[h],
-        )
+            at = pl.multiple_of((h * group + i * batch + n) * width, width)
+            out[:, pl.ds(at, width)] = done
 
     def attend(pair, first, last=False):
         blocks = [2 * pair, 2 * pair + 1]
@@ -316,9 +306,6 @@
                     summed[state] = summed[state] * rescale + o[:, :width]
                     total[state] = total[state] * rescale + o[:, width:]
 
-            if last:
-                leave(h).start()
-
     def await_over(pair):
         block = 2 * pair + 1 - side
 
@@ -367,10 +354,6 @@
             for i in range(group // batch):
                 state = (h, slice(i * batch * shard_rows, (i + 1) * batch * shard_rows))
                 finish(h, i, summed[state] * (1.0 / total[state]))
-            leave(h).start()
-
-    for h in range(kv_heads):
-        leave(h).wait()
 
     @pl.when(side == 0)
     def _():
@@ -418,9 +401,9 @@
     state = pltpu.VMEM((kv_heads, rows, width), jnp.float32)
     return pl.pallas_call(
         functools.partial(kernel, shards, width),
-        out_shape=jax.ShapeDtypeStruct(queries.shape, jnp.bfloat16),
+        out_shape=pltpu.VMEM(queries.shape, jnp.bfloat16),
         in_specs=[hbm] * 8,
-        out_specs=hbm,
+        out_specs=pl.BlockSpec(memory_space=pltpu.VMEM),
         scratch_shapes=[
             pltpu.VMEM(queries.shape, jnp.bfloat16),
             pltpu.VMEM(keys.shape, jnp.bfloat16),
@@ -439,8 +422,6 @@
             pltpu.SemaphoreType.DMA((shards, 2)),
             pltpu.SemaphoreType.DMA((shards, 2)),
             pltpu.SemaphoreType.DMA((8,)),
-            pltpu.VMEM((kv_heads, shard_rows, queries.shape[1] // kv_heads), jnp.bfloat16),
-            pltpu.SemaphoreType.DMA((kv_heads,)),
         ],
         compiler_params=pltpu.CompilerParams(
             collective_id=0, has_side_effects=True, vmem_limit_bytes=60 * 2**20

time: 25.4 us -> 23.5 us (0.925)
  local copies, waits for them, and re-layouts: 2.09 us -> 0.88 us
  Pallas kernels: 23.2 us -> 22.4 us
    unnamed x1, local copies, waits for them, and re-layouts: 2.09 us -> 0.88 us
    pallas_call x1, Pallas kernels: 23.2 us -> 22.4 us  [local(): pl.pallas_call(functools.partial(kernel, shards, width), out_shape=pltpu....]
where the time goes in v4:
time: 23.5 us; the launch traced here: 23.3 us
  Pallas kernels  22.4 us (95%)
  local copies, waits for them, and re-layouts  0.88 us (4%)
    pallas_call x1, Pallas kernels, local(): pl.pallas_call(functools.partial(kernel, shards, width), out_shape=pltpu....  22.4 us
    unnamed x1, local copies, waits for them, and re-layouts  0.88 us

profile of v4, /device:TPU:26, one launch (start us, length us, event | category | flops | bytes accessed | tf_op | source)
XLA Modules:
  0.0 23.3 jit_solution(12659059465325623890)
XLA Ops:
  0.0 22.4 %attend.1 = bf16[192,2048]{1,0:T(8,128)(2,1)S(1)} custom-call(bf16[192,2048]{1,0:T(8,128)(2,1)} %q_hbm.1, bf16[192,256]{1,0:T(8,128)(2,1)} %k_hbm.1, bf16[192,256]{1,0:T(8,128)(2,1)} %v_hbm.1, f32[1,128]{1,0:T(1,128)} %bitcast.2, f32[1,128]{1,0:T(1,128)} %bitcast.3, s32[8]{0:T(128)} %counts_hbm.1, f32[2,192,128]{2,1,0:T(8,128)} %constant.4.clone.inner_hbm, ...), custom_call_target="tpu_custom_call" | custom-call | tf_op jit(solution)/shard_map/attend/pallas_call | solution.py:402
  22.5 0.9 %copy.10 = bf16[192,2048]{1,0:T(8,128)(2,1)} copy(bf16[192,2048]{1,0:T(8,128)(2,1)S(1)} %attend.1) | data formatting | bytes 1572864

commit v5 on v4

--- a/solution.py
+++ b/solution.py
@@ -211,7 +211,9 @@
 
         to_over(block, VALUES).start()
 
-        to_up(block, KEYS).wait_recv()
+        @pl.when(not_last | (pair > 0))
+        def _():
+            to_up(block, KEYS).wait_recv()
 
         @pl.when(not_last)
         def _():
@@ -343,6 +345,10 @@
 
     @pl.when(not_first)
     def _():
+        @pl.when(level == levels - 1)
+        def _():
+            to_up(side, KEYS).wait_recv()
+
         detour()
         await_over(0)
         attend(0, False, True)

time: 23.5 us -> 23.5 us (level)
  no operation moved by 1% of the time
where the time goes in v5:
time: 23.5 us; the launch traced here: 23.3 us
  Pallas kernels  22.4 us (95%)
  local copies, waits for them, and re-layouts  0.88 us (4%)
    pallas_call x1, Pallas kernels, local(): pl.pallas_call(functools.partial(kernel, shards, width), out_shape=pltpu....  22.4 us
    unnamed x1, local copies, waits for them, and re-layouts  0.88 us

profile of v5, /device:TPU:26, one launch (start us, length us, event | category | flops | bytes accessed | tf_op | source)
XLA Modules:
  0.0 23.3 jit_solution(14465112881850190143)
XLA Ops:
  0.0 22.4 %attend.1 = bf16[192,2048]{1,0:T(8,128)(2,1)S(1)} custom-call(bf16[192,2048]{1,0:T(8,128)(2,1)} %q_hbm.1, bf16[192,256]{1,0:T(8,128)(2,1)} %k_hbm.1, bf16[192,256]{1,0:T(8,128)(2,1)} %v_hbm.1, f32[1,128]{1,0:T(1,128)} %bitcast.2, f32[1,128]{1,0:T(1,128)} %bitcast.3, s32[8]{0:T(128)} %counts_hbm.1, f32[2,192,128]{2,1,0:T(8,128)} %constant.4.clone.inner_hbm, ...), custom_call_target="tpu_custom_call" | custom-call | tf_op jit(solution)/shard_map/attend/pallas_call | solution.py:408
  22.5 0.9 %copy.10 = bf16[192,2048]{1,0:T(8,128)(2,1)} copy(bf16[192,2048]{1,0:T(8,128)(2,1)S(1)} %attend.1) | data formatting | bytes 1572864
